TPU v7x, 512 devices: a whole 4x4x16 slice. The times are simulated.
512 devices in a mesh: req: 32 (over z, core), seq: 16 (over x, y).
Axes of the slice: x: 4, y: 4, z: 16, core: 2. Of those that a mesh axis runs over, the one named last changes fastest.
Arguments:
- queries: bfloat16 [32768, 2560], P(('req', 'seq')), parts along dimension 0, may hold values from -30 to 30
- keys: bfloat16 [131072, 2560], P(('req', 'seq')), parts along dimension 0, may hold values from -30 to 30
- values: bfloat16 [131072, 2560], P(('req', 'seq')), parts along dimension 0, may hold values from -6 to 6
- active_blocks: int32 [256], P('req'), parts along dimension 0, may hold values from 0 to 31, as said below
Outputs:
- edited: bfloat16 [131072, 2560], P(('req', 'seq')), parts along dimension 0
There are 32 independent parts, one for each index of `req`. A program takes and returns all parts, laid end to end along the dimension named above; each array names one. Nothing has to cross between parts.
Inputs may be any that keep to these rules, and one draw needn't show every extreme that they name: `active_blocks`: distinct block numbers; block b holds tokens b * 128 to b * 128 + 127.
All inputs are finite; a program needn't handle non-finite values.
Results may differ from a plain program's by a relative error of at most 0.006.
Values may be sent and summed in bfloat16 or wider, within the bound.
A program may use at most 128 MiB of HBM per device.

v0:
```python
import jax
import jax.numpy as jnp
from jax import lax
from jax.sharding import PartitionSpec as P

HEADS = 20
HD = 128
BLK = 128
BPD = 2


def block_partials(query_rows, keys, values):
    row_count = query_rows.shape[0]
    key_count = keys.shape[0]
    query_heads = query_rows.reshape(row_count, HEADS, HD)
    key_heads = keys.reshape(key_count, HEADS, HD)
    value_heads = values.reshape(key_count, HEADS, HD)
    scores = jnp.einsum(
        "rhd,thd->hrt", query_heads, key_heads, preferred_element_type=jnp.float32
    ) * HD ** (-0.5)
    maxima = lax.optimization_barrier(jnp.max(scores, axis=-1).astype(jnp.bfloat16))
    shifted = jnp.exp(scores - maxima.astype(jnp.float32)[:, :, None])
    totals = jnp.sum(shifted, axis=-1).astype(jnp.bfloat16)
    weights = shifted.astype(jnp.bfloat16)
    numerators = jnp.einsum(
        "hrt,thd->rhd", weights, value_heads, preferred_element_type=jnp.float32
    )
    return (numerators.astype(jnp.bfloat16).reshape(row_count, HEADS * HD), maxima.T, totals.T)


def local(queries, keys, values, active_blocks):
    width = queries.shape[1]
    local_rows = queries.shape[0]
    group = lax.axis_size("seq")
    gathered = lax.all_gather(queries, "seq", axis=0, tiled=True)
    total_rows = gathered.shape[0]
    step_rows = min(512, total_rows)
    stacked = gathered.reshape(total_rows // step_rows, step_rows, width)
    numerators, maxima, totals = lax.map(lambda piece: block_partials(piece, keys, values), stacked)
    numerators = numerators.reshape(group, local_rows, width)
    maxima = maxima.reshape(group, local_rows, HEADS)
    totals = totals.reshape(group, local_rows, HEADS)
    numerators, maxima, totals = (
        lax.all_to_all(numerators, "seq", split_axis=0, concat_axis=0, tiled=True),
        lax.all_to_all(maxima, "seq", split_axis=0, concat_axis=0, tiled=True),
        lax.all_to_all(totals, "seq", split_axis=0, concat_axis=0, tiled=True),
    )
    maxima_f = maxima.astype(jnp.float32)
    highest = jnp.max(maxima_f, axis=0)
    factors = jnp.exp(maxima_f - highest[None])
    summed = jnp.sum(
        factors[:, :, :, None] * numerators.reshape(group, local_rows, HEADS, HD), axis=0
    )
    denominators = jnp.sum(factors * totals.astype(jnp.float32), axis=0)
    attended = (summed / denominators[:, :, None]).reshape(local_rows, width).astype(jnp.bfloat16)
    block_count = active_blocks.shape[0]
    returned = lax.all_gather(attended, "seq", axis=0, tiled=True)
    my_blocks = lax.axis_index("seq") * BPD + jnp.arange(BPD, dtype=jnp.int32)
    selector = (active_blocks[None, :] == my_blocks[:, None]).astype(jnp.bfloat16)
    listed = returned.reshape(block_count, BLK * width)
    edited = jnp.dot(selector, listed, preferred_element_type=jnp.float32).astype(jnp.bfloat16)
    return edited.reshape(BPD * BLK, width)


def solution(mesh):
    placed = (P(("req", "seq"), None), P(("req", "seq"), None), P(("req", "seq"), None), P("req"))
    return jax.shard_map(
        local, mesh=mesh, in_specs=placed, out_specs=P(("req", "seq"), None), check_vma=False
    )
```

profile of v0, /device:TPU:24, one launch (start us, length us, event | category | flops | bytes accessed | tf_op | source)
XLA Modules:
  0.0 317.3 jit_solution(11826227996479366936)
XLA Ops:
  6.5 0.0 all-gather.3.cloned.1.call-start
  6.5 0.7 all-gather.3.cloned.1.call-update
  7.3 2.4 copy.45
  9.7 2.5 copy.46
  12.2 74.1 %all-gather.3.cloned.1.call-done = bf16[1024,2560]{1,0:T(8,128)(2,1)} async-done(((bf16[64,2560]{1,0:T(8,128)(2,1)}), bf16[1024,2560]{1,0:T(8,128)(2,1)}) %all-gather.3.cloned.1.call-update) | async-done | bytes 5242896 | tf_op jit(solution)/shard_map/all_gather | solution.py:35
  86.3 37.1 %while.14 = (s32[]{:T(128)}, bf16[2,512,2560]{2,1,0:T(8,128)(2,1)}, bf16[2,512,20]{1,2,0:T(8,128)(2,1)S(1)}, bf16[2,512,20]{1,2,0:T(8,128)(2,1)S(1)}, bf16[2,512...) while((s32[]{:T(128)}, bf16[2,512,2560]{2,1,0:T(8,128)(2,1)}, ...), condition=%wide.region_3.4_spmd, body=%wide.region_0.3_spmd.sunk | while | flops 1364449280 | bytes 65819256 | solution.py:39
  86.3 1.9 constant_dynamic-slice_fusion.2
  88.2 2.6 copy.70
  90.8 3.7 %multiply_reduce_fusion.4 = (bf16[20,512]{1,0:T(8,128)(2,1)S(1)}, f32[20,512,256]{1,2,0:T(8,128)S(1)}) fusion(bf16[512,20,128]{0,2,1:T(8,128)(2,1)} %bitcast.57, bf16[256,20,128]{0,2,1:T(8,128)(2,1)} %bitcast.58), kind=kOutput, calls=%fused_computation.1.clone.1 | convolution fusion | flops 676321280 | bytes 14438400 | tf_op jit(solution)/shard_map/while/body/eval_jaxpr/rhd,thd->hrt/dot_general | solution.py:18
  94.6 0.0 copy-start
  94.6 1.9 fusion.29
  96.5 0.0 copy-done
  96.5 3.7 %fusion.28 = bf16[20,512,128]{1,2,0:T(8,128)(2,1)} fusion(bf16[256,20,128]{0,2,1:T(8,128)(2,1)S(1)} %bitcast.59, f32[20,512,256]{1,2,0:T(8,128)S(1)} %get-tuple-element.149, f32[20,512]{1,0:T(8,128)S(1)} %convert_element_type.62), kind=kOutput, calls=%fused_computation.7.clone.1 | convolution fusion | flops 680263680 | bytes 14458880 | tf_op jit(solution)/shard_map/while/body/eval_jaxpr/hrt,thd->rhd/dot_general | solution.py:25
  100.2 3.0 copy.71
  103.1 1.8 constant_dynamic-update-slice_fusion.2
  104.9 1.9 constant_dynamic-slice_fusion.2
  106.8 2.6 copy.70
  109.5 3.7 %multiply_reduce_fusion.4 = (bf16[20,512]{1,0:T(8,128)(2,1)S(1)}, f32[20,512,256]{1,2,0:T(8,128)S(1)}) fusion(bf16[512,20,128]{0,2,1:T(8,128)(2,1)} %bitcast.57, bf16[256,20,128]{0,2,1:T(8,128)(2,1)} %bitcast.58), kind=kOutput, calls=%fused_computation.1.clone.1 | convolution fusion | flops 676321280 | bytes 14438400 | tf_op jit(solution)/shard_map/while/body/eval_jaxpr/rhd,thd->hrt/dot_general | solution.py:18
  113.2 0.0 copy-start
  113.2 1.9 fusion.29
  115.1 0.0 copy-done
  115.1 3.7 %fusion.28 = bf16[20,512,128]{1,2,0:T(8,128)(2,1)} fusion(bf16[256,20,128]{0,2,1:T(8,128)(2,1)S(1)} %bitcast.59, f32[20,512,256]{1,2,0:T(8,128)S(1)} %get-tuple-element.149, f32[20,512]{1,0:T(8,128)S(1)} %convert_element_type.62), kind=kOutput, calls=%fused_computation.7.clone.1 | convolution fusion | flops 680263680 | bytes 14458880 | tf_op jit(solution)/shard_map/while/body/eval_jaxpr/hrt,thd->rhd/dot_general | solution.py:25
  118.8 3.0 copy.71
  121.8 1.7 constant_dynamic-update-slice_fusion.2
  123.5 0.1 reshape.49
  123.6 0.7 reshape.54
  124.4 5.7 %all-to-all-start = ((bf16[16,2,640]{2,1,0:T(2,128)(2,1)}), bf16[16,2,640]{2,1,0:T(2,128)(2,1)S(1)}, u32[]{:S(2)}, u32[]{:S(2)}) async-start(bf16[16,2,640]{2,1,0:T(2,128)(2,1)} %reshape.54), calls=%async_computation | async-start | bytes 81920 | tf_op jit(solution)/shard_map/all_to_all | solution.py:45
  130.1 0.1 reshape.51
  130.3 0.1 reshape.56
  130.4 5.4 %all-to-all-done = bf16[16,2,640]{2,1,0:T(2,128)(2,1)S(1)} async-done(((bf16[16,2,640]{2,1,0:T(2,128)(2,1)}), bf16[16,2,640]{2,1,0:T(2,128)(2,1)S(1)}, u32[]{:S(2)}, u32[]{:S(2)}) %all-to-all-start) | async-done | bytes 40992 | tf_op jit(solution)/shard_map/all_to_all | solution.py:45
  135.8 10.7 %all_to_all.15 = bf16[16,2,640]{2,1,0:T(2,128)(2,1)S(1)} all-to-all(bf16[16,2,640]{2,1,0:T(2,128)(2,1)S(1)} %reshape.56), channel_id=1, replica_groups=mesh['req'=32,'seq'=16] {'seq'}, dimensions={0} | all-to-all | bytes 81920 | tf_op jit(solution)/shard_map/all_to_all | solution.py:46
  146.5 6.4 %all-to-all-start.1 = ((bf16[16,64,2560]{2,1,0:T(8,128)(2,1)}), bf16[16,64,2560]{2,1,0:T(8,128)(2,1)}, u32[]{:S(2)}, u32[]{:S(2)}) async-start(bf16[16,64,2560]{2,1,0:T(8,128)(2,1)} %bitcast.61), calls=%async_computation.1 | async-start | bytes 10485760 | tf_op jit(solution)/shard_map/all_to_all | solution.py:44
  152.9 0.2 all-gather.5.cloned.1.call-start
  153.1 0.1 reshape.55
  153.3 0.1 reshape.57
  153.5 0.1 multiply_reduce_fusion.2
  153.5 0.2 copy.49
  153.8 7.1 %mul.21 = f32[16,64,20,128]{3,2,1,0:T(8,128)} broadcast(f32[16,64,20]{2,1,0:T(8,128)S(1)} %copy.49), dimensions={0,1,2} | broadcast | bytes 10567680 | tf_op jit(solution)/shard_map/mul | solution.py:52
  160.9 12.9 %mul.22 = f32[16,64,2560]{2,1,0:T(8,128)} reshape(f32[16,64,20,128]{3,2,1,0:T(8,128)} %mul.21) | data formatting | bytes 20971520 | tf_op jit(solution)/shard_map/mul | solution.py:52
  173.8 0.1 copy.54
  173.9 42.2 %all-to-all-done.1 = bf16[16,64,2560]{2,1,0:T(8,128)(2,1)} async-done(((bf16[16,64,2560]{2,1,0:T(8,128)(2,1)}), bf16[16,64,2560]{2,1,0:T(8,128)(2,1)}, u32[]{:S(2)}, u32[]{:S(2)}) %all-to-all-start.1) | async-done | bytes 5242912 | tf_op jit(solution)/shard_map/all_to_all | solution.py:44
  216.1 7.2 %multiply_reduce_fusion.1 = f32[64,2560]{1,0:T(8,128)S(1)} fusion(f32[16,64,2560]{2,1,0:T(8,128)} %mul.22, bf16[16,64,2560]{2,1,0:T(8,128)(2,1)} %all-to-all-done.1), kind=kLoop, calls=%fused_computation.14 | loop fusion | flops 7700480 | bytes 16384000 | tf_op jit(solution)/shard_map/reduce_sum | solution.py:51
  223.3 0.3 div.11
  223.6 0.9 fusion.10
  224.4 0.0 all-gather.5.cloned.1.call-update
  224.5 0.0 copy-start.1
  224.5 72.4 %all-gather.5.cloned.1.call-done = bf16[1024,2560]{1,0:T(8,128)(2,1)} async-done(((bf16[64,2560]{1,0:T(8,128)(2,1)}), bf16[1024,2560]{1,0:T(8,128)(2,1)}) %all-gather.5.cloned.1.call-update) | async-done | bytes 5242896 | tf_op jit(solution)/shard_map/all_gather | solution.py:57
  296.9 7.2 %reshape.52 = bf16[8,327680]{1,0:T(8,128)(2,1)} reshape(bf16[1024,2560]{1,0:T(8,128)(2,1)} %all-gather.5.cloned.1.call-done) | data formatting | bytes 10485760 | tf_op jit(solution)/shard_map/reshape | solution.py:60
  304.1 0.0 copy-done.1
  304.1 4.1 %convolution_convert_fusion = bf16[2,327680]{1,0:T(2,128)(2,1)S(1)} fusion(bf16[8,327680]{1,0:T(8,128)(2,1)} %reshape.52, s32[8]{0:T(128)S(1)} %copy-done.1, s32[2]{0:T(128)S(1)} %iota_add_fusion), kind=kOutput, calls=%fused_computation.13 | convolution fusion | flops 11141136 | bytes 6553640 | tf_op jit(solution)/shard_map/dot_general | solution.py:61
  308.2 2.3 reshape.53
  (14 shorter events, 0.2 us)
Async XLA Ops:
  6.5 79.8 %all-gather.3.cloned.1.call-start = ((), (), s32[]{:S(2)}) async-start(), calls=%async_computation.3 | async-start | bytes 5570560 | tf_op jit(solution)/shard_map/all_gather | solution.py:35
  94.6 1.9 copy-start
  113.2 1.9 copy-start
  124.4 11.4 %all-to-all-start = ((bf16[16,2,640]{2,1,0:T(2,128)(2,1)}), bf16[16,2,640]{2,1,0:T(2,128)(2,1)S(1)}, u32[]{:S(2)}, u32[]{:S(2)}) async-start(bf16[16,2,640]{2,1,0:T(2,128)(2,1)} %reshape.54), calls=%async_computation | async-start | bytes 81920 | tf_op jit(solution)/shard_map/all_to_all | solution.py:45
  146.5 69.6 %all-to-all-start.1 = ((bf16[16,64,2560]{2,1,0:T(8,128)(2,1)}), bf16[16,64,2560]{2,1,0:T(8,128)(2,1)}, u32[]{:S(2)}, u32[]{:S(2)}) async-start(bf16[16,64,2560]{2,1,0:T(8,128)(2,1)} %bitcast.61), calls=%async_computation.1 | async-start | bytes 10485760 | tf_op jit(solution)/shard_map/all_to_all | solution.py:44
  152.9 144.0 %all-gather.5.cloned.1.call-start = ((), (), s32[]{:S(2)}) async-start(), calls=%async_computation.4 | async-start | bytes 5570560 | tf_op jit(solution)/shard_map/all_gather | solution.py:57
  224.5 79.6 %copy-start.1 = (s32[8]{0:T(128)S(1)}, s32[8]{0:T(128)}, u32[]{:S(2)}) copy-start(s32[8]{0:T(128)} %param.9) | copy-start | bytes 100
Sparse Core Ops, SparseCore 0:
  10.4 75.8 all-gather.2
  224.6 72.2 all-gather.4
where the time goes:
time: 319 us; the launch traced here: 317 us
  waiting for transfers between devices  195 us (61%)
  local copies, waits for them, and re-layouts  55 us (17%)
  matrix products  18.8 us (6%)
  between operations  13.5 us (4%)
  starting transfers between devices  12.3 us (4%)
  other arithmetic  11.9 us (4%)
  blocking collectives  10.7 us (3%)
    all_gather x1, waiting for transfers between devices, local(): gathered = lax.all_gather(queries, 'seq', axis=0, tiled=True)  74.1 us
    all_gather x1, waiting for transfers between devices, local(): returned = lax.all_gather(attended, 'seq', axis=0, tiled=True)  72.4 us
    all_to_all x1, waiting for transfers between devices, local(): lax.all_to_all(numerators, 'seq', split_axis=0, concat_axis=0, tiled=True)  42.2 us
    mul x2, local copies, waits for them, and re-layouts, local(): factors[:, :, :, None] * numerators.reshape(group, local_rows, HEADS, HD)  20 us
    all_to_all x1, blocking collectives, local(): lax.all_to_all(totals, 'seq', split_axis=0, concat_axis=0, tiled=True)  10.7 us
    dynamic_update_slice x6, local copies, waits for them, and re-layouts, local(): lax.map(lambda piece: block_partials(piece, keys, values), stacked)  9.4 us
    dynamic_slice x4, local copies, waits for them, and re-layouts, local(): lax.map(lambda piece: block_partials(piece, keys, values), stacked)  9.09 us
    dot_general x2, matrix products, block_partials(): jnp.einsum('hrt,thd->rhd', weights, value_heads, preferred_element_type=j...  7.41 us
  transfers between devices with their start and end apart: 4, of which 4 were waited for; matrix products, arithmetic and copies ran while one was open for 8% of the time, Pallas kernels for 0%

commit v1 on v0

v1 whole, which is shorter than its diff:
```python
import jax
import jax.numpy as jnp
from jax import lax
from jax.experimental import pallas as pl
from jax.experimental.pallas import tpu as pltpu
from jax.sharding import PartitionSpec as P

HEADS = 20
HD = 128
BLK = 128
BPD = 2
SIDE = 4
OWN = HEADS // SIDE
ROWS = 64
TOK = 256
CHUNK = SIDE * ROWS
TOTAL = SIDE * CHUNK
GROUP = OWN * HD
SCALE = HD ** -0.5 * 1.4426950408889634
MESH = pl.DeviceIdType.MESH
OTHERS = (1, 3, 2)


def attend_head(h, qbuf, kbuf, vbuf, obuf, lbuf, eye, top):
    columns = pl.ds(pl.multiple_of(h * HD, HD), HD)
    for part in range(SIDE):
        rows = pl.ds(part * CHUNK, CHUNK)
        scores = lax.dot_general(
            qbuf[rows, columns], kbuf[h], (((1,), (1,)), ((), ())),
            preferred_element_type=jnp.float32,
        )
        high = jnp.max(scores, axis=-1, keepdims=True)
        weights = jnp.exp2((scores - high) * SCALE).astype(jnp.bfloat16)
        summed = jnp.dot(weights, vbuf[h], preferred_element_type=jnp.float32)
        totals = summed[:, HD:]
        obuf[h, rows, :] = (summed[:, :HD] / totals).astype(jnp.bfloat16)
        logs = high * SCALE + jnp.log2(totals)
        first = jnp.sum(jnp.where(eye, logs[:BLK], 0.0), axis=0, keepdims=True)
        second = jnp.sum(jnp.where(eye, logs[BLK:], 0.0), axis=0, keepdims=True)
        lbuf[h, part] = jnp.where(top, first, second)


def merge_head(h, obuf, lbuf, orecv, lrecv, att):
    logs = [lbuf[h, 0]] + [lrecv[h, i] for i in range(SIDE - 1)]
    highest = jnp.maximum(jnp.maximum(logs[0], logs[1]), jnp.maximum(logs[2], logs[3]))
    factors = [jnp.exp2(one - highest) for one in logs]
    inverse = 1.0 / (factors[0] + factors[1] + factors[2] + factors[3])
    for half in range(2):
        rows = slice(half * BLK, (half + 1) * BLK)
        total = None
        for i in range(SIDE):
            share = factors[i] * inverse
            spread = jnp.broadcast_to(share[half : half + 1, :], (BLK, HD)).T
            piece = obuf[h, rows, :] if i == 0 else orecv[h, i - 1, rows, :]
            term = spread * piece.astype(jnp.float32)
            total = term if total is None else total + term
        att[h, rows, :] = total.astype(jnp.bfloat16)


def kernel(
    act, q, k, v, out,
    qbuf, kbuf, vbuf, obuf, lbuf, orecv, lrecv, att, stage, pick,
    qs1, qr1, qs2, qr2, ks, kr, vs, vr, os, orr, ls, lr, as_, ar, ds, dr,
):
    core = lax.axis_index("req") % 2
    here = lax.axis_index("seq")
    x, y = here // SIDE, here % SIDE
    a = x + core * (y - x)
    b = y + core * (x - y)

    def device(da, db):
        ta, tb = (a + da) % SIDE, (b + db) % SIDE
        tx, ty = ta + core * (tb - ta), tb + core * (ta - tb)
        return tx * SIDE + ty

    def remote(src, dst, send, recv, da, db):
        return pltpu.make_async_remote_copy(
            src_ref=src, dst_ref=dst, send_sem=send, recv_sem=recv,
            device_id={"seq": device(da, db)}, device_id_type=MESH,
        )

    def group_columns(da):
        return pl.ds(pl.multiple_of((a + da) % SIDE * GROUP, GROUP), GROUP)

    def head_columns(da, h):
        return pl.ds(pl.multiple_of(((a + da) % SIDE * OWN + h) * HD, HD), HD)

    def query_local():
        return pltpu.make_async_copy(q.at[:, group_columns(0)], qbuf.at[pl.ds(0, ROWS)], qs1.at[0])

    def query_first(i):
        return remote(q.at[:, group_columns(i)], qbuf.at[pl.ds(i * ROWS, ROWS)], qs1.at[i], qr1.at[i], i, 0)

    def query_second(i):
        return remote(
            qbuf.at[pl.ds(0, CHUNK)], qbuf.at[pl.ds(i * CHUNK, CHUNK)], qs2.at[i], qr2.at[i], 0, i
        )

    def key_local(h):
        return pltpu.make_async_copy(k.at[:, head_columns(0, h)], kbuf.at[h, pl.ds(0, TOK)], ks.at[h, 0])

    def value_local(h):
        return pltpu.make_async_copy(
            v.at[:, head_columns(0, h)], vbuf.at[h, pl.ds(0, TOK), pl.ds(0, HD)], vs.at[h, 0]
        )

    def key_copy(h, i):
        return remote(
            k.at[:, head_columns(i, h)], kbuf.at[h, pl.ds(i * TOK, TOK)], ks.at[h, i], kr.at[h, i], i, 0
        )

    def value_copy(h, i):
        return remote(
            v.at[:, head_columns(i, h)], vbuf.at[h, pl.ds(i * TOK, TOK), pl.ds(0, HD)],
            vs.at[h, i], vr.at[h, i], i, 0,
        )

    def partial_copy(h, i):
        return remote(
            obuf.at[h, pl.ds((SIDE - i) * CHUNK, CHUNK)], orecv.at[h, i - 1],
            os.at[h, i], orr.at[h, i], 0, i,
        )

    def log_copy(h, i):
        return remote(lbuf.at[h, SIDE - i], lrecv.at[h, i - 1], ls.at[h, i], lr.at[h, i], 0, i)

    def merged_copy(h, i):
        return remote(
            att.at[h, pl.ds(0, CHUNK)], att.at[h, pl.ds(i * CHUNK, CHUNK)],
            as_.at[h, i], ar.at[h, i], 0, i,
        )

    def finished_local(h):
        return pltpu.make_async_copy(stage.at[h, 0], out.at[:, head_columns(0, h)], ds.at[h, 0])

    def finished_copy(h, i):
        return remote(stage.at[h, i], out.at[:, head_columns(0, h)], ds.at[h, i], dr.at[h, i], i, 0)

    barrier = pltpu.get_barrier_semaphore()
    for i in OTHERS:
        for da, db in ((i, 0), (0, i)):
            pl.semaphore_signal(barrier, inc=1, device_id={"seq": device(da, db)}, device_id_type=MESH)
    pl.semaphore_wait(barrier, 2 * len(OTHERS))

    query_local().start()
    for i in OTHERS:
        query_first(i).start()

    @pl.loop(0, OWN)
    def _(h):
        key_local(h).start()
        value_local(h).start()
        for i in OTHERS:
            key_copy(h, i).start()
            value_copy(h, i).start()

    @pl.loop(0, OWN)
    def _(h):
        vbuf[h, :, HD:] = jnp.ones((TOTAL, HD), jnp.bfloat16)

    query_local().wait()
    for i in OTHERS:
        query_first(i).wait()
    for i in OTHERS:
        query_second(i).start()
    for i in OTHERS:
        query_second(i).wait()

    line = lax.broadcasted_iota(jnp.int32, (BLK, HD), 0)
    eye = line == lax.broadcasted_iota(jnp.int32, (BLK, HD), 1)
    top = lax.broadcasted_iota(jnp.int32, (8, HD), 0) == 0

    pick[SIDE * SIDE] = jnp.zeros((ROWS, HD), jnp.bfloat16)
    places = []
    for owner in range(SIDE * SIDE):
        ox, oy = owner // SIDE, owner % SIDE
        oa, ob = ox + core * (oy - ox), oy + core * (ox - oy)
        places.append((b - ob + SIDE) % SIDE * SIDE + (a - oa + SIDE) % SIDE)
    sources = []
    for i in range(SIDE):
        wanted = []
        for slot in range(BPD):
            block = device(i, 0) * BPD + slot
            spots = [jnp.int32(SIDE * SIDE)] * 2
            for j in range(SIDE * SIDE // 2):
                match = act[j] == block
                spots = [jnp.where(match, places[2 * j + half], spots[half]) for half in range(2)]
            wanted += spots
        sources.append(wanted)

    @pl.loop(0, OWN + 2)
    def _(t):
        @pl.when(t < OWN)
        def _():
            key_local(t).wait()
            value_local(t).wait()
            for i in OTHERS:
                key_copy(t, i).wait()
                value_copy(t, i).wait()
            attend_head(t, qbuf, kbuf, vbuf, obuf, lbuf, eye, top)
            for i in OTHERS:
                partial_copy(t, i).start()
                log_copy(t, i).start()

        @pl.when((t >= 1) & (t < OWN + 1))
        def _():
            h = t - 1
            for i in OTHERS:
                partial_copy(h, i).wait()
                log_copy(h, i).wait()
            merge_head(h, obuf, lbuf, orecv, lrecv, att)
            for i in OTHERS:
                merged_copy(h, i).start()

        @pl.when(t >= 2)
        def _():
            h = t - 2
            for i in OTHERS:
                merged_copy(h, i).wait()
            for spot in range(SIDE * SIDE):
                pick[spot] = att[h, pl.ds(spot * ROWS, ROWS), :]
            for i in range(SIDE):
                for piece in range(2 * BPD):
                    stage[h, i, pl.ds(piece * ROWS, ROWS), :] = pick[sources[i][piece]]
            finished_local(h).start()
            for i in OTHERS:
                finished_copy(h, i).start()

    @pl.loop(0, OWN)
    def _(h):
        finished_local(h).wait()
        for i in OTHERS:
            finished_copy(h, i).wait()


def local(queries, keys, values, active_blocks):
    sems = pltpu.SemaphoreType.DMA
    bf16 = jnp.bfloat16
    return pl.pallas_call(
        kernel,
        out_shape=jax.ShapeDtypeStruct((TOK, HEADS * HD), bf16),
        in_specs=[pl.BlockSpec(memory_space=pltpu.SMEM)] + [pl.BlockSpec(memory_space=pl.ANY)] * 3,
        out_specs=pl.BlockSpec(memory_space=pl.ANY),
        scratch_shapes=[
            pltpu.VMEM((TOTAL, GROUP), bf16),
            pltpu.VMEM((OWN, TOTAL, HD), bf16),
            pltpu.VMEM((OWN, TOTAL, 2 * HD), bf16),
            pltpu.VMEM((OWN, TOTAL, HD), bf16),
            pltpu.VMEM((OWN, SIDE, 8, HD), jnp.float32),
            pltpu.VMEM((OWN, SIDE - 1, CHUNK, HD), bf16),
            pltpu.VMEM((OWN, SIDE - 1, 8, HD), jnp.float32),
            pltpu.VMEM((OWN, TOTAL, HD), bf16),
            pltpu.VMEM((OWN, SIDE, TOK, HD), bf16),
            pltpu.VMEM((SIDE * SIDE + 1, ROWS, HD), bf16),
        ]
        + [sems((SIDE,))] * 4
        + [sems((OWN, SIDE))] * 12,
        compiler_params=pltpu.CompilerParams(
            collective_id=0, has_side_effects=True, vmem_limit_bytes=48 * 2**20
        ),
        name="edit_attention",
    )(active_blocks, queries, keys, values)


def solution(mesh):
    placed = (P(("req", "seq"), None), P(("req", "seq"), None), P(("req", "seq"), None), P("req"))
    return jax.shard_map(
        local, mesh=mesh, in_specs=placed, out_specs=P(("req", "seq"), None), check_vma=False
    )
```

time: 319 us -> 72.2 us (0.23)
  waiting for transfers between devices: 195 us -> 0 us
  Pallas kernels: 0 us -> 66.1 us
  local copies, waits for them, and re-layouts: 55 us -> 5.32 us
  matrix products: 18.8 us -> 0 us
  between operations: 13.5 us -> 0.01 us
  starting transfers between devices: 12.3 us -> 0 us
  other arithmetic: 11.9 us -> 0 us
  blocking collectives: 10.7 us -> 0 us
    all_gather x2 -> x0, waiting for transfers between devices: 147 us -> none  [the longest x1 74.1 us: local(): gathered = lax.all_gather(queries, 'seq', axis=0, tiled=True)]
    pallas_call x0 -> x1, Pallas kernels: none -> 66.1 us  [local(): pl.pallas_call(kernel, out_shape=jax.ShapeDtypeStruct((TOK, HEADS * HD),...]
    all_to_all x2 -> x0, waiting for transfers between devices: 47.7 us -> none  [the longest x1 42.2 us: local(): lax.all_to_all(numerators, 'seq', split_axis=0, concat_axis=0, tiled=True)]
    mul x2 -> x0, local copies, waits for them, and re-layouts: 20 us -> none  [local(): factors[:, :, :, None] * numerators.reshape(group, local_rows, HEADS, HD)]
    dot_general x5 -> x0, matrix products: 18.8 us -> none  [the longest x2 7.41 us: block_partials(): jnp.einsum('hrt,thd->rhd', weights, value_heads, preferred_element_type=j...]
    all_to_all x2 -> x0, starting transfers between devices: 12.1 us -> none  [the longest x1 6.37 us: local(): lax.all_to_all(numerators, 'seq', split_axis=0, concat_axis=0, tiled=True)]
    reduce_sum x4 -> x0, other arithmetic: 10.9 us -> none  [the longest x1 7.16 us: local(): jnp.sum(factors[:, :, :, None] * numerators.reshape(group, local_rows, HE...]
    all_to_all x1 -> x0, blocking collectives: 10.7 us -> none  [local(): lax.all_to_all(totals, 'seq', split_axis=0, concat_axis=0, tiled=True)]
  transfers between devices with their start and end apart: 4 -> 0, of which waited for: 4 -> 0; matrix products, arithmetic and copies ran while one was open for 8% -> 0% of each run, Pallas kernels for 0% -> 0%
where the time goes in v1:
time: 72.2 us; the launch traced here: 71.4 us
  Pallas kernels  66.1 us (92%)
  local copies, waits for them, and re-layouts  5.32 us (7%)
    pallas_call x1, Pallas kernels, local(): pl.pallas_call(kernel, out_shape=jax.ShapeDtypeStruct((TOK, HEADS * HD),...  66.1 us
    unnamed x9, local copies, waits for them, and re-layouts  5.32 us

profile of v1, /device:TPU:24, one launch (start us, length us, event | category | flops | bytes accessed | tf_op | source)
XLA Modules:
  0.0 71.4 jit_solution(3374531707530156213)
XLA Ops:
  0.0 0.0 copy-start
  0.0 1.3 %copy-done = bf16[256,2560]{1,0:T(8,128)(2,1)S(1)} copy-done((bf16[256,2560]{1,0:T(8,128)(2,1)S(1)}, bf16[256,2560]{1,0:T(8,128)(2,1)}, u32[]{:S(2)}) %copy-start) | copy-done | bytes 1310744
  1.3 0.0 copy-start.1
  1.3 1.3 %copy-done.1 = bf16[256,2560]{1,0:T(8,128)(2,1)S(1)} copy-done((bf16[256,2560]{1,0:T(8,128)(2,1)S(1)}, bf16[256,2560]{1,0:T(8,128)(2,1)}, u32[]{:S(2)}) %copy-start.1) | copy-done | bytes 1310744
  2.6 0.0 copy-start.2
  2.6 1.0 %copy-done.2 = bf16[64,2560]{1,0:T(8,128)(2,1)S(1)} copy-done((bf16[64,2560]{1,0:T(8,128)(2,1)S(1)}, bf16[64,2560]{1,0:T(8,128)(2,1)}, u32[]{:S(2)}) %copy-start.2) | copy-done | bytes 327704
  3.6 0.0 copy-start.3
  3.6 0.7 copy-done.3
  4.3 66.1 %edit_attention.1 = bf16[256,2560]{1,0:T(8,128)(2,1)S(1)} custom-call(s32[8]{0:T(128)S(1)} %copy-done.3, bf16[64,2560]{1,0:T(8,128)(2,1)S(1)} %copy-done.2, bf16[256,2560]{1,0:T(8,128)(2,1)S(1)} %copy-done, bf16[256,2560]{1,0:T(8,128)(2,1)S(1)} %copy-done.1), custom_call_target="tpu_custom_call" | custom-call | tf_op jit(solution)/shard_map/edit_attention/pallas_call | solution.py:239
  70.3 1.1 %copy.6 = bf16[256,2560]{1,0:T(8,128)(2,1)} copy(bf16[256,2560]{1,0:T(8,128)(2,1)S(1)} %edit_attention.1) | data formatting | bytes 2621440
Async XLA Ops:
  0.0 1.3 %copy-start = (bf16[256,2560]{1,0:T(8,128)(2,1)S(1)}, bf16[256,2560]{1,0:T(8,128)(2,1)}, u32[]{:S(2)}) copy-start(bf16[256,2560]{1,0:T(8,128)(2,1)} %k.1) | copy-start | bytes 3932164
  1.3 1.3 %copy-start.1 = (bf16[256,2560]{1,0:T(8,128)(2,1)S(1)}, bf16[256,2560]{1,0:T(8,128)(2,1)}, u32[]{:S(2)}) copy-start(bf16[256,2560]{1,0:T(8,128)(2,1)} %v.1) | copy-start | bytes 3932164
  2.6 1.0 %copy-start.2 = (bf16[64,2560]{1,0:T(8,128)(2,1)S(1)}, bf16[64,2560]{1,0:T(8,128)(2,1)}, u32[]{:S(2)}) copy-start(bf16[64,2560]{1,0:T(8,128)(2,1)} %q.1) | copy-start | bytes 983044
  3.6 0.7 copy-start.3

commit v2 on v1

v2 whole, which is shorter than its diff:
```python
import jax
import jax.numpy as jnp
from jax import lax
from jax.experimental import pallas as pl
from jax.experimental.pallas import tpu as pltpu
from jax.sharding import PartitionSpec as P

HEADS = 20
HD = 128
BLK = 128
BPD = 2
SIDE = 4
GROUP = SIDE * SIDE
OWN = HEADS // SIDE
ROWS = 64
PIECE = ROWS // SIDE
TOK = 256
CHUNK = GROUP * PIECE
WIDTH = OWN * HD
SCALE = HD ** -0.5 * 1.4426950408889634
MESH = pl.DeviceIdType.MESH
OTHERS = (1, 3, 2)
REACHED = [(i // SIDE, i % SIDE) for i in range(1, GROUP)]
BF16 = jnp.bfloat16


def attend_head(h, qbuf, kbuf, vbuf, obuf, lbuf, eye, top):
    columns = pl.ds(pl.multiple_of(h * HD, HD), HD)
    for part in range(SIDE):
        scores = lax.dot_general(
            qbuf[part, :, :, columns].reshape(CHUNK, HD), kbuf[h], (((1,), (1,)), ((), ())),
            preferred_element_type=jnp.float32,
        )
        high = jnp.max(scores, axis=-1, keepdims=True)
        weights = jnp.exp2((scores - high) * SCALE).astype(BF16)
        summed = jnp.dot(weights, vbuf[h], preferred_element_type=jnp.float32)
        totals = summed[:, HD:]
        obuf[h, part] = (summed[:, :HD] / totals).astype(BF16)
        logs = high * SCALE + jnp.log2(totals)
        first = jnp.sum(jnp.where(eye, logs[:BLK], 0.0), axis=0, keepdims=True)
        second = jnp.sum(jnp.where(eye, logs[BLK:], 0.0), axis=0, keepdims=True)
        lbuf[h, part] = jnp.where(top, first, second)


def merge_head(h, mine, obuf, lbuf, orecv, lrecv, pick):
    logs = [lbuf[h, mine]] + [lrecv[h, i] for i in range(SIDE - 1)]
    highest = jnp.maximum(jnp.maximum(logs[0], logs[1]), jnp.maximum(logs[2], logs[3]))
    factors = [jnp.exp2(one - highest) for one in logs]
    inverse = 1.0 / (factors[0] + factors[1] + factors[2] + factors[3])
    for half in range(2):
        rows = slice(half * BLK, (half + 1) * BLK)
        total = None
        for i in range(SIDE):
            share = factors[i] * inverse
            spread = jnp.broadcast_to(share[half : half + 1, :], (BLK, HD)).T
            piece = obuf[h, mine, rows, :] if i == 0 else orecv[h, i - 1, rows, :]
            term = spread * piece.astype(jnp.float32)
            total = term if total is None else total + term
        spots = GROUP // 2
        pick[half * spots : (half + 1) * spots] = total.astype(BF16).reshape(spots, PIECE, HD)


def kernel(
    act, q, k, v, out,
    qbuf, kbuf, vbuf, obuf, lbuf, orecv, lrecv, pick, stage,
    q_own, q1s, q1r, q2s, q2r, own, ks, kr, vs, vr, os, orr, ls, lr, d_own, ds, dr,
):
    core = lax.axis_index("req") % 2
    here = lax.axis_index("seq")
    x, y = here // SIDE, here % SIDE
    a = x + core * (y - x)
    b = y + core * (x - y)

    def device(da, db):
        ta, tb = (a + da) % SIDE, (b + db) % SIDE
        tx, ty = ta + core * (tb - ta), tb + core * (ta - tb)
        return tx * SIDE + ty

    def remote(src, dst, send, recv, da, db):
        return pltpu.make_async_remote_copy(
            src_ref=src, dst_ref=dst, send_sem=send, recv_sem=recv,
            device_id={"seq": device(da, db)}, device_id_type=MESH,
        )

    def arrived(ref, send, recv):
        return remote(ref, ref, send, recv, 1, 0)

    def head_columns(da, h):
        return pl.ds(pl.multiple_of(((a + da) % SIDE * OWN + h) * HD, HD), HD)

    query_parts = ((0, HD), (HD, WIDTH - HD))

    def query_columns(da, n):
        start, size = query_parts[n]
        return pl.ds(pl.multiple_of((a + da) % SIDE * WIDTH + start, HD), size)

    def query_first(n, i):
        start, size = query_parts[n]
        source = q.at[:, :, query_columns(i, n)]
        target = qbuf.at[:, b * SIDE + i, :, pl.ds(start, size)]
        if i == 0:
            return pltpu.make_async_copy(source, target, q_own.at[n])
        return remote(source, target, q1s.at[n, i], q1r.at[n, i], i, 0)

    def query_second(n, i):
        start, size = query_parts[n]
        part = qbuf.at[:, pl.ds(b * SIDE, SIDE), :, pl.ds(start, size)]
        return remote(part, part, q2s.at[n, i], q2r.at[n, i], 0, i)

    def key_copy(h, i):
        source = k.at[:, head_columns(i, h)]
        target = kbuf.at[h, pl.ds(i * TOK, TOK)]
        if i == 0:
            return pltpu.make_async_copy(source, target, own.at[h, 0])
        return remote(source, target, ks.at[h], kr.at[h], i, 0)

    def value_copy(h, i):
        source = v.at[:, head_columns(i, h)]
        target = vbuf.at[h, pl.ds(i * TOK, TOK), pl.ds(0, HD)]
        if i == 0:
            return pltpu.make_async_copy(source, target, own.at[h, 1])
        return remote(source, target, vs.at[h], vr.at[h], i, 0)

    def partial_copy(h, i):
        return remote(obuf.at[h, (b + i) % SIDE], orecv.at[h, i - 1], os.at[h], orr.at[h], 0, i)

    def log_copy(h, i):
        return remote(lbuf.at[h, (b + i) % SIDE], lrecv.at[h, i - 1], ls.at[h], lr.at[h], 0, i)

    def finished_copy(h, n):
        target = out.at[:, b, :, head_columns(0, h)]
        if n == 0:
            return pltpu.make_async_copy(stage.at[h, 0], target, d_own.at[h])
        da, db = REACHED[n - 1]
        return remote(stage.at[h, n], target, ds.at[h], dr.at[h], da, db)

    barrier = pltpu.get_barrier_semaphore()
    for da, db in REACHED:
        pl.semaphore_signal(barrier, inc=1, device_id={"seq": device(da, db)}, device_id_type=MESH)
    pl.semaphore_wait(barrier, len(REACHED))

    def send_head(h):
        for i in OTHERS + (0,):
            key_copy(h, i).start()
        for i in OTHERS + (0,):
            value_copy(h, i).start()

    for i in OTHERS + (0,):
        query_first(0, i).start()
    send_head(0)
    for i in OTHERS + (0,):
        query_first(1, i).start()

    @pl.loop(1, OWN)
    def _(h):
        send_head(h)

    @pl.loop(0, OWN)
    def _(h):
        vbuf[h, :, HD:] = jnp.ones((SIDE * TOK, HD), BF16)

    for n in range(2):
        for i in OTHERS + (0,):
            query_first(n, i).wait()
        for i in OTHERS:
            query_second(n, i).start()

    pick[GROUP] = jnp.zeros((PIECE, HD), BF16)
    places = []
    for owner in range(GROUP):
        ox, oy = owner // SIDE, owner % SIDE
        oa, ob = ox + core * (oy - ox), oy + core * (ox - oy)
        places.append(ob * SIDE + (a - oa + SIDE) % SIDE)
    sources = []
    for n in range(GROUP):
        block = device(n // SIDE, n % SIDE) * BPD
        for slot in range(BPD):
            spots = [jnp.int32(GROUP)] * 2
            for j in range(GROUP // 2):
                match = act[j] == block + slot
                spots = [jnp.where(match, places[2 * j + half], spots[half]) for half in range(2)]
            sources += spots

    line = lax.broadcasted_iota(jnp.int32, (BLK, HD), 0)
    eye = line == lax.broadcasted_iota(jnp.int32, (BLK, HD), 1)
    top = lax.broadcasted_iota(jnp.int32, (8, HD), 0) == 0
    for i in OTHERS:
        query_second(0, i).wait()

    @pl.loop(0, OWN + 1)
    def _(t):
        @pl.when(t == 1)
        def _():
            for i in OTHERS:
                query_second(1, i).wait()

        @pl.when(t < OWN)
        def _():
            key_copy(t, 0).wait()
            value_copy(t, 0).wait()
            arrived(kbuf.at[t, pl.ds(TOK, 3 * TOK)], ks.at[t], kr.at[t]).wait()
            arrived(vbuf.at[t, pl.ds(TOK, 3 * TOK), pl.ds(0, HD)], vs.at[t], vr.at[t]).wait()
            attend_head(t, qbuf, kbuf, vbuf, obuf, lbuf, eye, top)
            for i in OTHERS:
                partial_copy(t, i).start()
                log_copy(t, i).start()

        @pl.when(t >= 1)
        def _():
            h = t - 1
            arrived(orecv.at[h], os.at[h], orr.at[h]).wait()
            arrived(lrecv.at[h], ls.at[h], lr.at[h]).wait()
            merge_head(h, b, obuf, lbuf, orecv, lrecv, pick)
            for n in range(GROUP):
                for piece in range(2 * BPD):
                    stage[h, n, piece] = pick[sources[2 * BPD * n + piece]]
                finished_copy(h, n).start()

    @pl.loop(0, OWN)
    def _(h):
        finished_copy(h, 0).wait()
        arrived(stage.at[h, pl.ds(1, GROUP - 1)], ds.at[h], dr.at[h]).wait()


def local(queries, keys, values, active_blocks):
    sems = pltpu.SemaphoreType.DMA
    width = HEADS * HD
    edited = pl.pallas_call(
        kernel,
        out_shape=jax.ShapeDtypeStruct((2 * BPD, SIDE, PIECE, width), BF16),
        in_specs=[pl.BlockSpec(memory_space=pltpu.SMEM)] + [pl.BlockSpec(memory_space=pl.ANY)] * 3,
        out_specs=pl.BlockSpec(memory_space=pl.ANY),
        scratch_shapes=[
            pltpu.VMEM((SIDE, GROUP, PIECE, WIDTH), BF16),
            pltpu.VMEM((OWN, SIDE * TOK, HD), BF16),
            pltpu.VMEM((OWN, SIDE * TOK, 2 * HD), BF16),
            pltpu.VMEM((OWN, SIDE, CHUNK, HD), BF16),
            pltpu.VMEM((OWN, SIDE, 8, HD), jnp.float32),
            pltpu.VMEM((OWN, SIDE - 1, CHUNK, HD), BF16),
            pltpu.VMEM((OWN, SIDE - 1, 8, HD), jnp.float32),
            pltpu.VMEM((GROUP + 1, PIECE, HD), BF16),
            pltpu.VMEM((OWN, GROUP, 2 * BPD, PIECE, HD), BF16),
        ]
        + [sems((2,))]
        + [sems((2, SIDE))] * 4
        + [sems((OWN, 2))]
        + [sems((OWN,))] * 11,
        compiler_params=pltpu.CompilerParams(
            collective_id=0, has_side_effects=True, vmem_limit_bytes=62 * 2**20
        ),
        name="edit_attention",
    )(active_blocks, queries.reshape(SIDE, PIECE, width), keys, values)
    return edited.reshape(TOK, width)


def solution(mesh):
    placed = (P(("req", "seq"), None), P(("req", "seq"), None), P(("req", "seq"), None), P("req"))
    return jax.shard_map(
        local, mesh=mesh, in_specs=placed, out_specs=P(("req", "seq"), None), check_vma=False
    )
```

time: 72.2 us -> 63.8 us (0.88)
  the two profiles are of different devices: /device:TPU:24 before, /device:TPU:288 now
where the time goes in v2:
time: 63.8 us; the launch traced here: 63.7 us
  Pallas kernels  61.2 us (96%)
  local copies, waits for them, and re-layouts  2.46 us (4%)
    pallas_call x1, Pallas kernels, local(): pl.pallas_call(kernel, out_shape=jax.ShapeDtypeStruct((2 * BPD, SIDE, PIE...  61.2 us
    unnamed x1, local copies, waits for them, and re-layouts  2.46 us

profile of v2, /device:TPU:288, one launch (start us, length us, event | category | flops | bytes accessed | tf_op | source)
XLA Modules:
  0.0 63.7 jit_solution(356257291929324793)
XLA Ops:
  0.0 61.2 %edit_attention.1 = bf16[4,4,16,2560]{3,2,1,0:T(8,128)(2,1)} custom-call(s32[8]{0:T(128)} %act.1, bf16[4,16,2560]{2,1,0:T(8,128)(2,1)} %bitcast.3, bf16[256,2560]{1,0:T(8,128)(2,1)} %k.1, bf16[256,2560]{1,0:T(8,128)(2,1)} %v.1), custom_call_target="tpu_custom_call" | custom-call | tf_op jit(solution)/shard_map/edit_attention/pallas_call | solution.py:228
  61.2 2.5 %copy.6 = bf16[256,2560]{1,0:T(8,128)(2,1)} copy(bf16[256,2560]{1,0:T(8,128)(2,1)} %bitcast.2) | data formatting | bytes 2621440

commit v3 on v2

--- a/solution.py
+++ b/solution.py
@@ -20,6 +20,7 @@
 SCALE = HD ** -0.5 * 1.4426950408889634
 MESH = pl.DeviceIdType.MESH
 OTHERS = (1, 3, 2)
+LAG = 3
 REACHED = [(i // SIDE, i % SIDE) for i in range(1, GROUP)]
 BF16 = jnp.bfloat16
 
@@ -65,7 +66,7 @@
     qbuf, kbuf, vbuf, obuf, lbuf, orecv, lrecv, pick, stage,
     q_own, q1s, q1r, q2s, q2r, own, ks, kr, vs, vr, os, orr, ls, lr, d_own, ds, dr,
 ):
-    core = lax.axis_index("req") % 2
+    core = 1 - lax.axis_index("req") % 2
     here = lax.axis_index("seq")
     x, y = here // SIDE, here % SIDE
     a = x + core * (y - x)
@@ -187,7 +188,7 @@
     for i in OTHERS:
         query_second(0, i).wait()
 
-    @pl.loop(0, OWN + 1)
+    @pl.loop(0, OWN + LAG)
     def _(t):
         @pl.when(t == 1)
         def _():
@@ -205,9 +206,9 @@
                 partial_copy(t, i).start()
                 log_copy(t, i).start()
 
-        @pl.when(t >= 1)
+        @pl.when(t >= LAG)
         def _():
-            h = t - 1
+            h = t - LAG
             arrived(orecv.at[h], os.at[h], orr.at[h]).wait()
             arrived(lrecv.at[h], ls.at[h], lr.at[h]).wait()
             merge_head(h, b, obuf, lbuf, orecv, lrecv, pick)
@@ -227,7 +228,7 @@
     width = HEADS * HD
     edited = pl.pallas_call(
         kernel,
-        out_shape=jax.ShapeDtypeStruct((2 * BPD, SIDE, PIECE, width), BF16),
+        out_shape=pltpu.VMEM((2 * BPD, SIDE, PIECE, width), BF16),
         in_specs=[pl.BlockSpec(memory_space=pltpu.SMEM)] + [pl.BlockSpec(memory_space=pl.ANY)] * 3,
         out_specs=pl.BlockSpec(memory_space=pl.ANY),
         scratch_shapes=[

time: 63.8 us -> 59.6 us (0.934)
  the two profiles are of different devices: /device:TPU:288 before, /device:TPU:448 now
where the time goes in v3:
time: 59.6 us; the launch traced here: 59.5 us
  Pallas kernels  58.5 us (98%)
  local copies, waits for them, and re-layouts  1.06 us (2%)
    pallas_call x1, Pallas kernels, local(): pl.pallas_call(kernel, out_shape=pltpu.VMEM((2 * BPD, SIDE, PIECE, width)...  58.5 us

profile of v3, /device:TPU:448, one launch (start us, length us, event | category | flops | bytes accessed | tf_op | source)
XLA Modules:
  0.0 59.5 jit_solution(716750745913134714)
XLA Ops:
  0.0 58.5 %edit_attention.1 = bf16[4,4,16,2560]{3,2,1,0:T(8,128)(2,1)S(1)} custom-call(s32[8]{0:T(128)} %act.1, bf16[4,16,2560]{2,1,0:T(8,128)(2,1)} %bitcast.3, bf16[256,2560]{1,0:T(8,128)(2,1)} %k.1, bf16[256,2560]{1,0:T(8,128)(2,1)} %v.1), custom_call_target="tpu_custom_call" | custom-call | tf_op jit(solution)/shard_map/edit_attention/pallas_call | solution.py:229
  58.5 1.1 %copy.6 = bf16[256,2560]{1,0:T(8,128)(2,1)} copy(bf16[256,2560]{1,0:T(8,128)(2,1)S(1)} %bitcast.2) | data formatting | bytes 2621440

commit v4 on v3

--- a/solution.py
+++ b/solution.py
@@ -19,8 +19,8 @@
 WIDTH = OWN * HD
 SCALE = HD ** -0.5 * 1.4426950408889634
 MESH = pl.DeviceIdType.MESH
-OTHERS = (1, 3, 2)
-LAG = 3
+OTHERS = (2, 1, 3)
+FARTHEST_FIRST = (10, 6, 9, 14, 11, 5, 15, 7, 13, 2, 8, 1, 4, 3, 12, 0)
 REACHED = [(i // SIDE, i % SIDE) for i in range(1, GROUP)]
 BF16 = jnp.bfloat16
 
@@ -188,7 +188,9 @@
     for i in OTHERS:
         query_second(0, i).wait()
 
-    @pl.loop(0, OWN + LAG)
+    lag = 2 + core
+
+    @pl.loop(0, OWN + 3)
     def _(t):
         @pl.when(t == 1)
         def _():
@@ -206,13 +208,13 @@
                 partial_copy(t, i).start()
                 log_copy(t, i).start()
 
-        @pl.when(t >= LAG)
+        @pl.when((t >= lag) & (t < OWN + lag))
         def _():
-            h = t - LAG
+            h = t - lag
             arrived(orecv.at[h], os.at[h], orr.at[h]).wait()
             arrived(lrecv.at[h], ls.at[h], lr.at[h]).wait()
             merge_head(h, b, obuf, lbuf, orecv, lrecv, pick)
-            for n in range(GROUP):
+            for n in FARTHEST_FIRST:
                 for piece in range(2 * BPD):
                     stage[h, n, piece] = pick[sources[2 * BPD * n + piece]]
                 finished_copy(h, n).start()

time: 59.6 us -> 59 us (0.990)
  the two profiles are of different devices: /device:TPU:448 before, /device:TPU:24 now
where the time goes in v4:
time: 59 us; the launch traced here: 58.8 us
  Pallas kernels  57.8 us (98%)
  local copies, waits for them, and re-layouts  1.06 us (2%)
    pallas_call x1, Pallas kernels, local(): pl.pallas_call(kernel, out_shape=pltpu.VMEM((2 * BPD, SIDE, PIECE, width)...  57.8 us

profile of v4, /device:TPU:24, one launch (start us, length us, event | category | flops | bytes accessed | tf_op | source)
XLA Modules:
  0.0 58.8 jit_solution(9102868519638706493)
XLA Ops:
  0.0 57.8 %edit_attention.1 = bf16[4,4,16,2560]{3,2,1,0:T(8,128)(2,1)S(1)} custom-call(s32[8]{0:T(128)} %act.1, bf16[4,16,2560]{2,1,0:T(8,128)(2,1)} %bitcast.3, bf16[256,2560]{1,0:T(8,128)(2,1)} %k.1, bf16[256,2560]{1,0:T(8,128)(2,1)} %v.1), custom_call_target="tpu_custom_call" | custom-call | tf_op jit(solution)/shard_map/edit_attention/pallas_call | solution.py:231
  57.8 1.1 %copy.6 = bf16[256,2560]{1,0:T(8,128)(2,1)} copy(bf16[256,2560]{1,0:T(8,128)(2,1)S(1)} %bitcast.2) | data formatting | bytes 2621440

commit v5 on v4

--- a/solution.py
+++ b/solution.py
@@ -152,19 +152,20 @@
     for i in OTHERS + (0,):
         query_first(1, i).start()
 
-    @pl.loop(1, OWN)
-    def _(h):
-        send_head(h)
-
-    @pl.loop(0, OWN)
-    def _(h):
-        vbuf[h, :, HD:] = jnp.ones((SIDE * TOK, HD), BF16)
-
     for n in range(2):
         for i in OTHERS + (0,):
             query_first(n, i).wait()
         for i in OTHERS:
             query_second(n, i).start()
+        if n == 0:
+
+            @pl.loop(1, OWN)
+            def _(h):
+                send_head(h)
+
+            @pl.loop(0, OWN)
+            def _(h):
+                vbuf[h, :, HD:] = jnp.ones((SIDE * TOK, HD), BF16)
 
     pick[GROUP] = jnp.zeros((PIECE, HD), BF16)
     places = []
@@ -188,7 +189,7 @@
     for i in OTHERS:
         query_second(0, i).wait()
 
-    lag = 2 + core
+    lag = 2
 
     @pl.loop(0, OWN + 3)
     def _(t):

time: 59 us -> 58.8 us (level); the launches traced: 58.8 us -> 58 us
  Pallas kernels: 57.8 us -> 57 us
    pallas_call x1, Pallas kernels: 57.8 us -> 57 us  [local(): pl.pallas_call(kernel, out_shape=pltpu.VMEM((2 * BPD, SIDE, PIECE, width)...]
where the time goes in v5:
time: 58.8 us; the launch traced here: 58 us
  Pallas kernels  57 us (97%)
  local copies, waits for them, and re-layouts  1.06 us (2%)
    pallas_call x1, Pallas kernels, local(): pl.pallas_call(kernel, out_shape=pltpu.VMEM((2 * BPD, SIDE, PIECE, width)...  57 us

profile of v5, /device:TPU:24, one launch (start us, length us, event | category | flops | bytes accessed | tf_op | source)
XLA Modules:
  0.0 58.0 jit_solution(6475247723313663332)
XLA Ops:
  0.0 57.0 %edit_attention.1 = bf16[4,4,16,2560]{3,2,1,0:T(8,128)(2,1)S(1)} custom-call(s32[8]{0:T(128)} %act.1, bf16[4,16,2560]{2,1,0:T(8,128)(2,1)} %bitcast.3, bf16[256,2560]{1,0:T(8,128)(2,1)} %k.1, bf16[256,2560]{1,0:T(8,128)(2,1)} %v.1), custom_call_target="tpu_custom_call" | custom-call | tf_op jit(solution)/shard_map/edit_attention/pallas_call | solution.py:232
  57.0 1.1 %copy.6 = bf16[256,2560]{1,0:T(8,128)(2,1)} copy(bf16[256,2560]{1,0:T(8,128)(2,1)S(1)} %bitcast.2) | data formatting | bytes 2621440

commit v6 on v5

--- a/solution.py
+++ b/solution.py
@@ -37,9 +37,12 @@
         summed = jnp.dot(weights, vbuf[h], preferred_element_type=jnp.float32)
         totals = summed[:, HD:]
         obuf[h, part] = (summed[:, :HD] / totals).astype(BF16)
-        logs = high * SCALE + jnp.log2(totals)
-        first = jnp.sum(jnp.where(eye, logs[:BLK], 0.0), axis=0, keepdims=True)
-        second = jnp.sum(jnp.where(eye, logs[BLK:], 0.0), axis=0, keepdims=True)
+        packed = []
+        for rows in (slice(0, BLK), slice(BLK, CHUNK)):
+            most = jnp.sum(jnp.where(eye, high[rows], 0.0), axis=0, keepdims=True)
+            count = jnp.sum(jnp.where(eye, totals[rows], 0.0), axis=0, keepdims=True)
+            packed.append(most * SCALE + jnp.log2(count))
+        first, second = packed
         lbuf[h, part] = jnp.where(top, first, second)
 
 

time: 58.8 us -> 59.1 us (level)
  no operation moved by 1% of the time
where the time goes in v6:
time: 59.1 us; the launch traced here: 58 us
  Pallas kernels  57 us (96%)
  local copies, waits for them, and re-layouts  1.06 us (2%)
    pallas_call x1, Pallas kernels, local(): pl.pallas_call(kernel, out_shape=pltpu.VMEM((2 * BPD, SIDE, PIECE, width)...  57 us

profile of v6, /device:TPU:24, one launch (start us, length us, event | category | flops | bytes accessed | tf_op | source)
XLA Modules:
  0.0 58.0 jit_solution(18345029222279200422)
XLA Ops:
  0.0 57.0 %edit_attention.1 = bf16[4,4,16,2560]{3,2,1,0:T(8,128)(2,1)S(1)} custom-call(s32[8]{0:T(128)} %act.1, bf16[4,16,2560]{2,1,0:T(8,128)(2,1)} %bitcast.3, bf16[256,2560]{1,0:T(8,128)(2,1)} %k.1, bf16[256,2560]{1,0:T(8,128)(2,1)} %v.1), custom_call_target="tpu_custom_call" | custom-call | tf_op jit(solution)/shard_map/edit_attention/pallas_call | solution.py:235
  57.0 1.1 %copy.6 = bf16[256,2560]{1,0:T(8,128)(2,1)} copy(bf16[256,2560]{1,0:T(8,128)(2,1)S(1)} %bitcast.2) | data formatting | bytes 2621440
